TPU v7x, 256 devices: a whole 4x4x8 slice. The times are simulated.
256 devices in a mesh: gx: 16 (over y, x_hi, core), gy: 16 (over x_lo, z).
Axes of the slice: x: 4 (x_hi: 2, x_lo: 2; x = x_hi * 2 + x_lo), y: 4, z: 8, core: 2. Of those that a mesh axis runs over, the one named last changes fastest.
Arguments:
- east_flow: float32 [8, 2048, 8192], P(None, 'gx', 'gy'), may hold values from -36 to 36
- north_flow: float32 [8, 2048, 8192], P(None, 'gx', 'gy'), may hold values from -36 to 36
Outputs:
- stress: float32 [3, 8, 512, 2048], P(None, None, 'gx', 'gy')
- library: float32 [48, 8, 512, 2048], P(None, None, 'gx', 'gy')
All inputs are finite; a program needn't handle non-finite values.
Results may differ from a plain program's by a relative error of at most 0.0003.
Values sent between devices are 32-bit elements; how exact they have to be, the bound alone decides.
A program may use at most 128 MiB of HBM per device.

v0:
```python
import jax
import jax.numpy as jnp
from jax import lax
from jax.sharding import PartitionSpec as P

spread_cells = 5.5


def with_halo(block, sides, width):
    for axis, dim in sides:
        count = lax.axis_size(axis)
        forward = [(i, i + 1) for i in range(count - 1)]
        forward.append((count - 1, 0))
        backward = [(target, source) for source, target in forward]
        low = lax.ppermute(
            lax.slice_in_dim(block, block.shape[dim] - width, None, axis=dim), axis, forward
        )
        high = lax.ppermute(lax.slice_in_dim(block, 0, width, axis=dim), axis, backward)
        block = jnp.concatenate([low, block, high], axis=dim)
    return block


def band_matrix(count_out, count_in):
    offsets = jnp.arange(33).astype(jnp.float32) - 16.0
    total = jnp.sum(jnp.exp(-0.5 * (offsets / spread_cells) ** 2))
    lag = jnp.arange(count_in)[None, :] - 4 * jnp.arange(count_out)[:, None]
    lagged = lag.astype(jnp.float32) - 16.0
    values = jnp.exp(-0.5 * (lagged / spread_cells) ** 2) / total
    return jnp.where((lag >= 0) & (lag <= 32), values, jnp.float32(0.0))


def first_form(plus_two, plus_one, minus_one, minus_two):
    return (8.0 * plus_one - plus_two - 8.0 * minus_one + minus_two) / 12.0


def second_form(plus_two, plus_one, centre, minus_one, minus_two):
    return (16.0 * plus_one - plus_two - 30.0 * centre + 16.0 * minus_one - minus_two) / 12.0


def moved(field, step, axis):
    count = field.shape[axis] - 4
    return lax.slice_in_dim(field, 2 + step, 2 + step + count, axis=axis)


def first_diff(field, axis):
    return first_form(
        moved(field, 2, axis), moved(field, 1, axis), moved(field, -1, axis), moved(field, -2, axis)
    )


def second_diff(field, axis):
    return second_form(
        moved(field, 2, axis),
        moved(field, 1, axis),
        moved(field, 0, axis),
        moved(field, -1, axis),
        moved(field, -2, axis),
    )


def build_library(
    east_mean,
    north_mean,
    grad_ux,
    grad_uy,
    grad_vx,
    grad_vy,
    curve_uxx,
    curve_uxy,
    curve_uyy,
    curve_vxx,
    curve_vxy,
    curve_vyy,
):
    vorticity = grad_vx - grad_uy
    features = [
        grad_ux,
        grad_uy,
        grad_vx,
        grad_vy,
        curve_uxx,
        curve_uxy,
        curve_uyy,
        curve_vxx,
        curve_vxy,
        curve_vyy,
        curve_vxx - curve_uxy,
        curve_vxy - curve_uyy,
    ]
    columns = []
    for feature in features:
        columns.append(feature)
        columns.append(east_mean * feature)
        columns.append(north_mean * feature)
        columns.append(vorticity * feature)
    return jnp.stack(columns, axis=0)


def with_products(pair):
    east, north = (pair[0], pair[1])
    return jnp.stack([east, north, east * east, east * north, north * north], axis=0)


def smooth_rows(fields, matrix):
    return jnp.einsum("cp,flpq->flcq", matrix, fields, precision=lax.Precision.HIGHEST)


def smooth_cols(fields, matrix):
    return jnp.einsum("flcq,dq->flcd", fields, matrix, precision=lax.Precision.HIGHEST)


def per_device(east_flow, north_flow):
    levels, count_x, count_y = east_flow.shape
    rows_matrix = band_matrix(count_x // 4, count_x + 32)
    cols_matrix = band_matrix(count_y // 4, count_y + 32)
    outgoing = with_products(jnp.stack([east_flow, north_flow], axis=0))
    arrived = with_halo(outgoing, (("gx", 2), ("gy", 3)), 16)
    means = smooth_cols(smooth_rows(arrived, rows_matrix), cols_matrix)
    east_mean, north_mean = (means[0], means[1])
    stress = jnp.stack(
        [
            means[2] - east_mean * east_mean,
            means[3] - east_mean * north_mean,
            means[4] - north_mean * north_mean,
        ],
        axis=0,
    )
    rim = with_halo(jnp.stack([east_mean, north_mean], axis=0), (("gx", 2), ("gy", 3)), 2)
    inner_x = lax.slice_in_dim(rim, 2, rim.shape[2] - 2, axis=2)
    along_x = first_diff(rim, 2)
    grad_x = lax.slice_in_dim(along_x, 2, along_x.shape[3] - 2, axis=3)
    grad_y = first_diff(inner_x, 3)
    curve_xx_full = second_diff(rim, 2)
    curve_xx = lax.slice_in_dim(curve_xx_full, 2, curve_xx_full.shape[3] - 2, axis=3)
    curve_yy = second_diff(inner_x, 3)
    curve_xy = first_diff(along_x, 3)
    library = build_library(
        east_mean,
        north_mean,
        grad_x[0],
        grad_y[0],
        grad_x[1],
        grad_y[1],
        curve_xx[0],
        curve_xy[0],
        curve_yy[0],
        curve_xx[1],
        curve_xy[1],
        curve_yy[1],
    )
    return (stress, library)


def solution(mesh):
    return jax.shard_map(
        per_device,
        mesh=mesh,
        in_specs=(P(None, "gx", "gy"), P(None, "gx", "gy")),
        out_specs=(P(None, None, "gx", "gy"), P(None, None, "gx", "gy")),
        check_vma=False,
    )
```

profile of v0, /device:TPU:1, one launch (start us, length us, event | category | flops | bytes accessed | tf_op | source)
XLA Modules:
  0.0 118.0 jit_solution(9005194056582805598)
XLA Ops:
  0.7 2.0 %bitcast_dynamic-update-slice_fusion.4 = f32[5,8,128,512]{3,2,1,0:T(8,128)S(1)} fusion(f32[8,128,512]{2,1,0:T(8,128)} %param.2), kind=kLoop, calls=%fused_computation.19 | loop fusion | bytes 4194304
  2.6 1.8 %bitcast_dynamic-update-slice_fusion.3 = f32[5,8,128,512]{3,2,1,0:T(8,128)S(1)} fusion(f32[5,8,128,512]{3,2,1,0:T(8,128)S(1)} %bitcast_dynamic-update-slice_fusion.4, f32[8,128,512]{2,1,0:T(8,128)} %param.3), kind=kLoop, calls=%fused_computation.18 | loop fusion | bytes 4194304
  4.5 0.2 bitcast_dynamic-update-slice_fusion.2
  4.7 0.5 bitcast_dynamic-update-slice_fusion.1
  5.2 0.2 bitcast_dynamic-update-slice_fusion
  5.5 0.2 fusion.75
  5.7 4.2 %collective-permute-start = (f32[5,8,16,512]{3,2,1,0:T(8,128)S(1)}, f32[5,8,16,512]{3,2,1,0:T(8,128)S(1)}, u32[]{:S(2)}, u32[]{:S(2)}) collective-permute-start(f32[5,8,16,512]{3,2,1,0:T(8,128)S(1)} %get-tuple-element.10), channel_id=1, source_target_pairs={{0,16},{16,32},{32,48},{48,64},{64,80},{80,96},{96,112},{112,128},... | collective-permute-start | bytes 3932168 | tf_op jit(solution)/shard_map/ppermute | solution.py:15
  9.9 23.9 %collective-permute-done = f32[5,8,16,512]{3,2,1,0:T(8,128)S(1)} collective-permute-done((f32[5,8,16,512]{3,2,1,0:T(8,128)S(1)}, f32[5,8,16,512]{3,2,1,0:T(8,128)S(1)}, u32[]{:S(2)}, u32[]{:S(2)}) %collective-permute-start) | collective-permute-done | bytes 1310752 | tf_op jit(solution)/shard_map/ppermute | solution.py:15
  33.8 6.7 %collective-permute-done.1 = f32[5,8,16,512]{3,2,1,0:T(8,128)S(1)} collective-permute-done((f32[5,8,16,512]{3,2,1,0:T(8,128)S(1)}, f32[5,8,16,512]{3,2,1,0:T(8,128)S(1)}, u32[]{:S(2)}, u32[]{:S(2)}) %collective-permute-start.1) | collective-permute-done | bytes 1310752 | tf_op jit(solution)/shard_map/ppermute | solution.py:18
  40.5 4.2 %pad_maximum_fusion.2 = (f32[5,8,160,16]{3,2,1,0:T(8,128)}, f32[5,8,160,16]{3,2,1,0:T(8,128)}) fusion(f32[5,8,16,512]{3,2,1,0:T(8,128)S(1)} %collective-permute-done.1, f32[5,8,128,512]{3,2,1,0:T(8,128)S(1)} %bitcast_dynamic-update-slice_fusion, f32[5,8,16,512]{3,2,1,0:T(8,128)S(1)} %collective-permute-done), kind=kLoop, calls=%fused_computation.12 | loop fusion | flops 409600 | bytes 13926400 | tf_op jit(solution)/shard_map/slice | solution.py:16
  44.7 2.9 %copy.12 = f32[5,8,160,16]{2,3,1,0:T(8,128)S(1)} copy(f32[5,8,160,16]{3,2,1,0:T(8,128)} %get-tuple-element.8) | data formatting | bytes 819200 | tf_op jit(solution)/shard_map/slice | solution.py:16
  47.5 1.4 %collective-permute-start.2 = (f32[5,8,160,16]{2,3,1,0:T(8,128)S(1)}, f32[5,8,160,16]{2,3,1,0:T(8,128)S(1)}, u32[]{:S(2)}, u32[]{:S(2)}) collective-permute-start(f32[5,8,160,16]{2,3,1,0:T(8,128)S(1)} %copy.12), channel_id=1, source_target_pairs={{0,1},{1,2},{2,3},{3,4},{4,5},{5,6},{6,7},{7,8},{8,9},{9,10},{10,1... | collective-permute-start | bytes 1228808 | tf_op jit(solution)/shard_map/ppermute | solution.py:15
  49.0 2.8 %copy.13 = f32[5,8,160,16]{2,3,1,0:T(8,128)S(1)} copy(f32[5,8,160,16]{3,2,1,0:T(8,128)} %get-tuple-element.9) | data formatting | bytes 819200 | tf_op jit(solution)/shard_map/slice | solution.py:18
  51.8 5.1 %collective-permute-start.3 = (f32[5,8,160,16]{2,3,1,0:T(8,128)S(1)}, f32[5,8,160,16]{2,3,1,0:T(8,128)S(1)}, u32[]{:S(2)}, u32[]{:S(2)}) collective-permute-start(f32[5,8,160,16]{2,3,1,0:T(8,128)S(1)} %copy.13), channel_id=1, source_target_pairs={{1,0},{2,1},{3,2},{4,3},{5,4},{6,5},{7,6},{8,7},{9,8},{10,9},{11,1... | collective-permute-start | bytes 1228808 | tf_op jit(solution)/shard_map/ppermute | solution.py:18
  57.0 0.6 exponential_reduce_fusion
  57.6 10.4 %collective-permute-done.2 = f32[5,8,160,16]{2,3,1,0:T(8,128)S(1)} collective-permute-done((f32[5,8,160,16]{2,3,1,0:T(8,128)S(1)}, f32[5,8,160,16]{2,3,1,0:T(8,128)S(1)}, u32[]{:S(2)}, u32[]{:S(2)}) %collective-permute-start.2) | collective-permute-done | bytes 409632 | tf_op jit(solution)/shard_map/ppermute | solution.py:15
  68.0 2.4 %copy.14 = f32[5,8,160,16]{3,2,1,0:T(8,128)} copy(f32[5,8,160,16]{2,3,1,0:T(8,128)S(1)} %collective-permute-done.2) | data formatting | bytes 819200 | tf_op jit(solution)/shard_map/ppermute | solution.py:15
  70.4 0.6 collective-permute-done.3
  70.9 2.3 %copy.15 = f32[5,8,160,16]{3,2,1,0:T(8,128)} copy(f32[5,8,160,16]{2,3,1,0:T(8,128)S(1)} %collective-permute-done.3) | data formatting | bytes 819200 | tf_op jit(solution)/shard_map/ppermute | solution.py:18
  73.2 18.2 %fusion = f32[5,8,544,32]{2,3,1,0:T(8,128)S(1)} fusion(f32[5,8,160,16]{3,2,1,0:T(8,128)} %copy.15, f32[5,8,16,512]{3,2,1,0:T(8,128)} %copy-done.4, f32[5,8,128,512]{3,2,1,0:T(8,128)} %copy-done, f32[5,8,16,512]{3,2,1,0:T(8,128)} %copy-done.3, f32[5,8,160,16]{3,2,1,0:T(8,128)} %copy.14, f32[]{:T(128)} %exponential_reduce_fusion, s32[32]{0:T(128)S(1)} %iota_multiply_fusion.1), kind=kOutput, calls=%fused_computation | convolution fusion | flops 1350917120 | bytes 16711812 | tf_op jit(solution)/shard_map/cp,flpq->flcq/dot_general | solution.py:105
  91.4 3.5 %fusion.10 = f32[5,8,32,128]{3,2,1,0:T(8,128)S(1)} fusion(f32[5,8,544,32]{2,3,1,0:T(8,128)S(1)} %fusion, f32[]{:T(128)} %exponential_reduce_fusion, s32[128]{0:T(128)S(1)} %iota_multiply_fusion), kind=kOutput, calls=%fused_computation.13 | convolution fusion | flops 1070313472 | bytes 3441156 | tf_op jit(solution)/shard_map/flcq,dq->flcd/dot_general | solution.py:109
  95.0 0.5 collective-permute-start.4
  95.4 0.1 collective-permute-start.5
  95.6 0.7 collective-permute-done.4
  96.3 4.1 %collective-permute-done.5 = f32[2,8,2,128]{3,2,1,0:T(2,128)S(1)} collective-permute-done((f32[2,8,2,128]{3,2,1,0:T(2,128)S(1)}, f32[2,8,2,128]{3,2,1,0:T(2,128)S(1)}, u32[]{:S(2)}, u32[]{:S(2)}) %collective-permute-start.5) | collective-permute-done | bytes 16416 | tf_op jit(solution)/shard_map/ppermute | solution.py:18
  100.5 0.2 fusion.77
  100.7 3.7 %collective-permute-start.7 = (f32[2,8,36,2]{3,2,1,0:T(8,128)S(1)}, f32[2,8,36,2]{3,2,1,0:T(8,128)S(1)}, u32[]{:S(2)}, u32[]{:S(2)}) collective-permute-start(f32[2,8,36,2]{3,2,1,0:T(8,128)S(1)} %get-tuple-element.21), channel_id=1, source_target_pairs={{1,0},{2,1},{3,2},{4,3},{5,4},{6,5},{7,6},{8,7},{9,8},{10,9},{11,1... | collective-permute-start | bytes 13832 | tf_op jit(solution)/shard_map/ppermute | solution.py:18
  104.4 5.8 %collective-permute-done.6 = f32[2,8,36,2]{3,2,1,0:T(8,128)S(1)} collective-permute-done((f32[2,8,36,2]{3,2,1,0:T(8,128)S(1)}, f32[2,8,36,2]{3,2,1,0:T(8,128)S(1)}, u32[]{:S(2)}, u32[]{:S(2)}) %collective-permute-start.6) | collective-permute-done | bytes 4640 | tf_op jit(solution)/shard_map/ppermute | solution.py:15
  110.2 0.4 pad_maximum_fusion.3
  110.6 0.4 fusion.15
  111.1 0.3 fusion.30
  111.4 0.1 multiply_dynamic-update-slice_fusion.35
  111.5 0.1 multiply_dynamic-update-slice_fusion.34
  111.6 0.6 add_multiply_fusion.1
  112.2 0.1 multiply_dynamic-update-slice_fusion.33
  112.6 0.1 multiply_dynamic-update-slice_fusion.29
  112.7 0.1 multiply_dynamic-update-slice_fusion.28
  112.8 0.1 multiply_dynamic-update-slice_fusion.27
  113.1 0.1 multiply_dynamic-update-slice_fusion.23
  113.2 0.1 multiply_dynamic-update-slice_fusion.22
  113.3 0.1 multiply_dynamic-update-slice_fusion.21
  113.5 0.6 subtract_multiply_fusion
  114.3 0.1 multiply_dynamic-update-slice_fusion.14
  114.4 0.1 multiply_dynamic-update-slice_fusion.13
  114.5 0.1 multiply_dynamic-update-slice_fusion.12
  114.9 0.1 constant_dynamic-update-slice_fusion.1
  115.2 0.8 pad_maximum_fusion.4
  116.1 2.0 %copy-done.5 = f32[48,8,32,128]{3,2,1,0:T(8,128)} copy-done((f32[48,8,32,128]{3,2,1,0:T(8,128)}, f32[48,8,32,128]{3,2,1,0:T(8,128)S(1)}, u32[]{:S(2)}) %copy-start.5) | copy-done | bytes 6291480
  (54 shorter events, 1.2 us)
Async XLA Ops:
  0.6 3.9 %copy-start.1 = (f32[8,128,512]{2,1,0:T(8,128)S(1)}, f32[8,128,512]{2,1,0:T(8,128)}, u32[]{:S(2)}) copy-start(f32[8,128,512]{2,1,0:T(8,128)} %param.2) | copy-start | bytes 6291460
  0.6 4.1 %copy-start.2 = (f32[8,128,512]{2,1,0:T(8,128)S(1)}, f32[8,128,512]{2,1,0:T(8,128)}, u32[]{:S(2)}) copy-start(f32[8,128,512]{2,1,0:T(8,128)} %param.3) | copy-start | bytes 6291460
  5.5 39.2 %copy-start = (f32[5,8,128,512]{3,2,1,0:T(8,128)}, f32[5,8,128,512]{3,2,1,0:T(8,128)S(1)}, u32[]{:S(2)}) copy-start(f32[5,8,128,512]{3,2,1,0:T(8,128)S(1)} %bitcast_dynamic-update-slice_fusion) | copy-start | bytes 31457284
  5.7 28.1 %collective-permute-start = (f32[5,8,16,512]{3,2,1,0:T(8,128)S(1)}, f32[5,8,16,512]{3,2,1,0:T(8,128)S(1)}, u32[]{:S(2)}, u32[]{:S(2)}) collective-permute-start(f32[5,8,16,512]{3,2,1,0:T(8,128)S(1)} %get-tuple-element.10), channel_id=1, source_target_pairs={{0,16},{16,32},{32,48},{48,64},{64,80},{80,96},{96,112},{112,128},... | collective-permute-start | bytes 3932168 | tf_op jit(solution)/shard_map/ppermute | solution.py:15
  9.9 30.6 %collective-permute-start.1 = (f32[5,8,16,512]{3,2,1,0:T(8,128)S(1)}, f32[5,8,16,512]{3,2,1,0:T(8,128)S(1)}, u32[]{:S(2)}, u32[]{:S(2)}) collective-permute-start(f32[5,8,16,512]{3,2,1,0:T(8,128)S(1)} %get-tuple-element.11), channel_id=1, source_target_pairs={{16,0},{32,16},{48,32},{64,48},{80,64},{96,80},{112,96},{128,112},... | collective-permute-start | bytes 3932168 | tf_op jit(solution)/shard_map/ppermute | solution.py:18
  33.8 10.9 %copy-start.3 = (f32[5,8,16,512]{3,2,1,0:T(8,128)}, f32[5,8,16,512]{3,2,1,0:T(8,128)S(1)}, u32[]{:S(2)}) copy-start(f32[5,8,16,512]{3,2,1,0:T(8,128)S(1)} %collective-permute-done) | copy-start | bytes 3932164
  40.5 4.2 %copy-start.4 = (f32[5,8,16,512]{3,2,1,0:T(8,128)}, f32[5,8,16,512]{3,2,1,0:T(8,128)S(1)}, u32[]{:S(2)}) copy-start(f32[5,8,16,512]{3,2,1,0:T(8,128)S(1)} %collective-permute-done.1) | copy-start | bytes 3932164
  47.5 20.4 %collective-permute-start.2 = (f32[5,8,160,16]{2,3,1,0:T(8,128)S(1)}, f32[5,8,160,16]{2,3,1,0:T(8,128)S(1)}, u32[]{:S(2)}, u32[]{:S(2)}) collective-permute-start(f32[5,8,160,16]{2,3,1,0:T(8,128)S(1)} %copy.12), channel_id=1, source_target_pairs={{0,1},{1,2},{2,3},{3,4},{4,5},{5,6},{6,7},{7,8},{8,9},{9,10},{10,1... | collective-permute-start | bytes 1228808 | tf_op jit(solution)/shard_map/ppermute | solution.py:15
  51.8 19.1 %collective-permute-start.3 = (f32[5,8,160,16]{2,3,1,0:T(8,128)S(1)}, f32[5,8,160,16]{2,3,1,0:T(8,128)S(1)}, u32[]{:S(2)}, u32[]{:S(2)}) collective-permute-start(f32[5,8,160,16]{2,3,1,0:T(8,128)S(1)} %copy.13), channel_id=1, source_target_pairs={{1,0},{2,1},{3,2},{4,3},{5,4},{6,5},{7,6},{8,7},{9,8},{10,9},{11,1... | collective-permute-start | bytes 1228808 | tf_op jit(solution)/shard_map/ppermute | solution.py:18
  95.0 1.3 %collective-permute-start.4 = (f32[2,8,2,128]{3,2,1,0:T(2,128)S(1)}, f32[2,8,2,128]{3,2,1,0:T(2,128)S(1)}, u32[]{:S(2)}, u32[]{:S(2)}) collective-permute-start(f32[2,8,2,128]{3,2,1,0:T(2,128)S(1)} %get-tuple-element.18), channel_id=1, source_target_pairs={{0,16},{16,32},{32,48},{48,64},{64,80},{80,96},{96,112},{112,128},... | collective-permute-start | bytes 49160 | tf_op jit(solution)/shard_map/ppermute | solution.py:15
  95.4 5.0 %collective-permute-start.5 = (f32[2,8,2,128]{3,2,1,0:T(2,128)S(1)}, f32[2,8,2,128]{3,2,1,0:T(2,128)S(1)}, u32[]{:S(2)}, u32[]{:S(2)}) collective-permute-start(f32[2,8,2,128]{3,2,1,0:T(2,128)S(1)} %get-tuple-element.19), channel_id=1, source_target_pairs={{16,0},{32,16},{48,32},{64,48},{80,64},{96,80},{112,96},{128,112},... | collective-permute-start | bytes 49160 | tf_op jit(solution)/shard_map/ppermute | solution.py:18
  100.6 9.6 %collective-permute-start.6 = (f32[2,8,36,2]{3,2,1,0:T(8,128)S(1)}, f32[2,8,36,2]{3,2,1,0:T(8,128)S(1)}, u32[]{:S(2)}, u32[]{:S(2)}) collective-permute-start(f32[2,8,36,2]{3,2,1,0:T(8,128)S(1)} %get-tuple-element.20), channel_id=1, source_target_pairs={{0,1},{1,2},{2,3},{3,4},{4,5},{5,6},{6,7},{7,8},{8,9},{9,10},{10,1... | collective-permute-start | bytes 13832 | tf_op jit(solution)/shard_map/ppermute | solution.py:15
  100.7 9.5 %collective-permute-start.7 = (f32[2,8,36,2]{3,2,1,0:T(8,128)S(1)}, f32[2,8,36,2]{3,2,1,0:T(8,128)S(1)}, u32[]{:S(2)}, u32[]{:S(2)}) collective-permute-start(f32[2,8,36,2]{3,2,1,0:T(8,128)S(1)} %get-tuple-element.21), channel_id=1, source_target_pairs={{1,0},{2,1},{3,2},{4,3},{5,4},{6,5},{7,6},{8,7},{9,8},{10,9},{11,1... | collective-permute-start | bytes 13832 | tf_op jit(solution)/shard_map/ppermute | solution.py:18
  115.2 2.8 %copy-start.5 = (f32[48,8,32,128]{3,2,1,0:T(8,128)}, f32[48,8,32,128]{3,2,1,0:T(8,128)S(1)}, u32[]{:S(2)}) copy-start(f32[48,8,32,128]{3,2,1,0:T(8,128)S(1)} %multiply_dynamic-update-slice_fusion) | copy-start | bytes 18874372
where the time goes:
time: 119 us; the launch traced here: 118 us
  waiting for transfers between devices  52.2 us (44%)
  matrix products  21.7 us (18%)
  local copies, waits for them, and re-layouts  17 us (14%)
  starting transfers between devices  15.2 us (13%)
  other arithmetic  10.8 us (9%)
    ppermute x4, waiting for transfers between devices, with_halo(): lax.ppermute(lax.slice_in_dim(block, block.shape[dim] - width, None, axis...  40.8 us
    dot_general x1, matrix products, smooth_rows(): jnp.einsum('cp,flpq->flcq', matrix, fields, precision=lax.Precision.HIGHEST)  18.2 us
    ppermute x4, waiting for transfers between devices, with_halo(): lax.ppermute(lax.slice_in_dim(block, 0, width, axis=dim), axis, backward)  11.4 us
    ppermute x4, starting transfers between devices, with_halo(): lax.ppermute(lax.slice_in_dim(block, 0, width, axis=dim), axis, backward)  8.98 us
    unnamed x24, local copies, waits for them, and re-layouts  6.23 us
    ppermute x4, starting transfers between devices, with_halo(): lax.ppermute(lax.slice_in_dim(block, block.shape[dim] - width, None, axis...  6.17 us
    slice x1, other arithmetic, with_halo(): lax.slice_in_dim(block, block.shape[dim] - width, None, axis=dim)  4.18 us
    dot_general x1, matrix products, smooth_cols(): jnp.einsum('flcq,dq->flcd', fields, matrix, precision=lax.Precision.HIGHEST)  3.53 us
  transfers between devices with their start and end apart: 8, of which 7 were waited for; matrix products, arithmetic and copies ran while one was open for 5% of the time, Pallas kernels for 0%

commit v1 on v0

v1 whole, which is shorter than its diff:
```python
import jax
import jax.numpy as jnp
import ml_dtypes
import numpy as np
from jax import lax
from jax.experimental import pallas as pl
from jax.experimental.pallas import tpu as pltpu
from jax.sharding import PartitionSpec as P

spread_cells = 5.5
MESH = pl.DeviceIdType.MESH

LEV, FX, FY = 8, 128, 512
CX, CY = FX // 4, FY // 4
ROWS = CX + 8
PAIR = 2
CHUNKS = LEV // PAIR
COMBOS = 5 * PAIR
TILES = 8


def gauss_taps():
    offsets = np.arange(33, dtype=np.float32) - np.float32(16.0)
    bumps = np.exp(np.float32(-0.5) * (offsets / np.float32(spread_cells)) ** 2)
    return (bumps / np.sum(bumps)).astype(np.float32)


def two_pieces(values):
    high = values.astype(ml_dtypes.bfloat16)
    low = (values - high.astype(np.float32)).astype(ml_dtypes.bfloat16)
    return high, low


def row_factor():
    taps = gauss_taps()
    band = np.zeros((ROWS, FX), np.float32)
    for at in range(ROWS):
        for p in range(FX):
            lag = p - 4 * (at - 4) + 16
            if 0 <= lag <= 32:
                band[at, p] = taps[lag]
    high, low = two_pieces(band)
    return np.concatenate(
        [np.concatenate([high, high], axis=1), np.concatenate([low, low], axis=1)], axis=0
    )


def column_factor():
    taps = gauss_taps()
    half = FY // 2
    blocks = []
    for part in range(2):
        band = np.zeros((half, CY), np.float32)
        for c in range(-4, CY + 4):
            for p in range(half):
                lag = p + part * half - 4 * c + 16
                if 0 <= lag <= 32:
                    band[p, c % CY] = taps[lag]
        high, low = two_pieces(band)
        blocks.append(np.concatenate([high, low], axis=1))
    return np.stack(blocks, axis=0)


def split(values):
    high = values.astype(jnp.bfloat16)
    low = (values - high.astype(jnp.float32)).astype(jnp.bfloat16)
    return high, low


def turn(values, lanes):
    return pltpu.roll(values, lanes % CY, 1)


def filter_kernel(
    east, north, rows_hbm, cols_hbm, means, rims,
    fine, rows_w, cols_w, half_done, edges,
    to_y, to_x, from_y, from_c, from_x,
    load_sem, send_sem, recv_sem,
):
    here_x, here_y = lax.axis_index("gx"), lax.axis_index("gy")
    count_x, count_y = lax.axis_size("gx"), lax.axis_size("gy")
    up, down = lax.rem(here_x + 1, count_x), lax.rem(here_x + count_x - 1, count_x)
    right, left = lax.rem(here_y + 1, count_y), lax.rem(here_y + count_y - 1, count_y)
    neighbours = [
        (here_x, right), (here_x, left), (down, here_y), (up, here_y),
        (down, right), (up, right), (down, left), (up, left),
    ]

    barrier = pltpu.get_barrier_semaphore()
    for neighbour in neighbours:
        pl.semaphore_signal(barrier, inc=1, device_id=neighbour, device_id_type=MESH)

    def load(level, which):
        source = east if which == 0 else north
        return pltpu.make_async_copy(
            source.at[level], fine.at[which, level], load_sem.at[which, level]
        )

    rows_copy = pltpu.make_async_copy(rows_hbm, rows_w, load_sem.at[0, LEV])
    cols_copy = pltpu.make_async_copy(cols_hbm, cols_w, load_sem.at[1, LEV])
    rows_copy.start()
    load(0, 0).start()
    load(0, 1).start()
    cols_copy.start()

    def start_load(level, carry):
        load(level, 0).start()
        load(level, 1).start()
        return carry

    lax.fori_loop(1, LEV, start_load, 0)

    def sends(k):
        pieces = [
            (to_y.at[k, 0], from_y.at[k, 0]),
            (to_y.at[k, 1], from_y.at[k, 1]),
            (to_x.at[k, 0], from_x.at[k, 0]),
            (to_x.at[k, 1], from_x.at[k, 1]),
            (to_y.at[k, 0, pl.ds(0, 8)], from_c.at[k, 0]),
            (to_y.at[k, 0, pl.ds(CX, 8)], from_c.at[k, 1]),
            (to_y.at[k, 1, pl.ds(0, 8)], from_c.at[k, 2]),
            (to_y.at[k, 1, pl.ds(CX, 8)], from_c.at[k, 3]),
        ]
        return [
            pltpu.make_async_remote_copy(
                src_ref=source, dst_ref=target,
                send_sem=send_sem.at[k, n], recv_sem=recv_sem.at[k, n],
                device_id=neighbours[n], device_id_type=MESH,
            )
            for n, (source, target) in enumerate(pieces)
        ]

    rows_copy.wait()
    cols_copy.wait()
    pl.semaphore_wait(barrier, len(neighbours))

    lane = lax.broadcasted_iota(jnp.int32, (ROWS, CY), 1)
    group = lane // 8
    spot = lane % 8
    sub = lax.broadcasted_iota(jnp.int32, (8, CY), 0)

    def chunk(k, carry):
        for j in range(PAIR):
            level = PAIR * k + j
            load(level, 0).wait()
            load(level, 1).wait()
            u = fine[0, level]
            v = fine[1, level]
            for f, values in enumerate((u, v, u * u, u * v, v * v)):
                high, low = split(values)
                both = jnp.dot(
                    rows_w[...], jnp.concatenate([high, low], axis=0),
                    preferred_element_type=jnp.float32,
                )
                half_done[pl.ds((5 * j + f) * ROWS, ROWS), :] = both[:ROWS] + both[ROWS:]
        parts = []
        for part in range(2):
            high, low = split(half_done[:, part * (FY // 2):(part + 1) * (FY // 2)])
            weights = cols_w[part]
            both = jnp.dot(
                jnp.concatenate([high, low], axis=1),
                jnp.concatenate([weights, weights], axis=0),
                preferred_element_type=jnp.float32,
            )
            parts.append(both[:, :CY] + both[:, CY:])
        packed_main = jnp.zeros((ROWS, CY), jnp.float32)
        packed_edge = jnp.zeros((ROWS, CY), jnp.float32)
        for n in range(COMBOS):
            j, f = n // 5, n % 5
            first = parts[0][n * ROWS:(n + 1) * ROWS]
            second = parts[1][n * ROWS:(n + 1) * ROWS]
            main = jnp.where(lane < CY - 4, first, 0.0) + jnp.where(lane >= 4, second, 0.0)
            edge = jnp.where(lane >= CY // 2, first, second)
            means[PAIR * k + j, f] = main
            packed_edge = jnp.where(group == n, turn(edge, 8 * n + 4), packed_edge)
            if f < 2:
                packed_main = jnp.where(group == n, turn(main, 8 * n + 4), packed_main)
        edges[k] = packed_edge
        to_y[k, 0] = jnp.where(spot >= 4, packed_edge, packed_main)
        to_y[k, 1] = jnp.where(spot < 4, packed_edge, packed_main)
        for side in range(2):
            at = side * CX
            keep = (sub < 4) if side == 0 else (sub >= 4)

            def rows_of(j, f):
                return means[PAIR * k + j, f, pl.ds(at, 8)]

            for j in range(PAIR):
                to_x[k, side, 2 * j] = rows_of(j, 0)
                to_x[k, side, 2 * j + 1] = rows_of(j, 1)
                to_x[k, side, 4 + j] = jnp.where(
                    keep, rows_of(j, 2), pltpu.roll(rows_of(j, 3), 4, 0)
                )
            to_x[k, side, 6] = jnp.where(keep, rows_of(0, 4), pltpu.roll(rows_of(1, 4), 4, 0))
            to_x[k, side, 7] = packed_edge[at:at + 8]
        for copy in sends(k):
            copy.start()
        return carry

    lax.fori_loop(0, CHUNKS, chunk, 0)

    def join(k, carry):
        for copy in sends(k):
            copy.wait_recv()
        spans = ((0, 8), (8, CX - 8), (CX, 8))
        for at, size in spans:
            rows = pl.ds(at, size)
            from_left = from_y[k, 0, rows]
            from_right = from_y[k, 1, rows]
            own = edges[k, rows]
            if at == 0:
                from_left = from_left + from_c[k, 1]
                from_right = from_right + from_c[k, 3]
                own = own + from_x[k, 1, 7]
            if at == CX:
                from_left = from_left + from_c[k, 0]
                from_right = from_right + from_c[k, 2]
                own = own + from_x[k, 0, 7]
            near = spot[:size] >= 4
            inward = jnp.where(near, from_left, from_right)
            outward = jnp.where(near, from_right, from_left) + own
            lanes = lane[:size]
            inside = (lanes < 4) | (lanes >= CY - 4)
            for n in range(COMBOS):
                j, f = n // 5, n % 5
                level = PAIR * k + j
                total = means[level, f, rows] + jnp.where(inside, turn(inward, -8 * n - 4), 0.0)
                if at != 8:
                    side = 1 if at == 0 else 0
                    if f < 2:
                        total = total + from_x[k, side, 2 * j + f]
                    else:
                        slot = 4 + j if f < 4 else 6
                        tile = from_x[k, side, slot]
                        second_half = f == 3 or (f == 4 and j == 1)
                        total = total + (pltpu.roll(tile, 4, 0) if second_half else tile)
                means[level, f, rows] = total
                if f < 2:
                    rims[level, f, rows] = turn(outward, -8 * n - 4)
        return carry

    lax.fori_loop(0, CHUNKS, join, 0)

    def finish(k, carry):
        for copy in sends(k):
            copy.wait_send()
        return carry

    lax.fori_loop(0, CHUNKS, finish, 0)


def filtered(east_flow, north_flow):
    dma = pltpu.SemaphoreType.DMA
    anywhere = pl.BlockSpec(memory_space=pltpu.HBM)
    inside = pl.BlockSpec(memory_space=pltpu.VMEM)
    f32, bf16 = jnp.float32, jnp.bfloat16
    return pl.pallas_call(
        filter_kernel,
        out_shape=(
            jax.ShapeDtypeStruct((LEV, 5, ROWS, CY), f32),
            jax.ShapeDtypeStruct((LEV, 2, ROWS, CY), f32),
        ),
        in_specs=[anywhere] * 4,
        out_specs=(inside, inside),
        scratch_shapes=[
            pltpu.VMEM((2, LEV, FX, FY), f32),
            pltpu.VMEM((2 * ROWS, 2 * FX), bf16),
            pltpu.VMEM((2, FY // 2, 2 * CY), bf16),
            pltpu.VMEM((COMBOS * ROWS, FY), f32),
            pltpu.VMEM((CHUNKS, ROWS, CY), f32),
            pltpu.VMEM((CHUNKS, 2, ROWS, CY), f32),
            pltpu.VMEM((CHUNKS, 2, TILES, 8, CY), f32),
            pltpu.VMEM((CHUNKS, 2, ROWS, CY), f32),
            pltpu.VMEM((CHUNKS, 4, 8, CY), f32),
            pltpu.VMEM((CHUNKS, 2, TILES, 8, CY), f32),
            dma((2, LEV + 1)),
            dma((CHUNKS, 8)),
            dma((CHUNKS, 8)),
        ],
        compiler_params=pltpu.CompilerParams(
            collective_id=0, has_side_effects=True, vmem_limit_bytes=32 * 1024 * 1024
        ),
        name="filter_and_exchange",
    )(
        *[
            pltpu.with_memory_space_constraint(array, pltpu.HBM)
            for array in (
                east_flow, north_flow, jnp.asarray(row_factor()), jnp.asarray(column_factor())
            )
        ]
    )


def first_form(plus_two, plus_one, minus_one, minus_two):
    return (8.0 * (plus_one - minus_one) - (plus_two - minus_two)) * (1.0 / 12.0)


def second_form(plus_two, plus_one, centre, minus_one, minus_two):
    return (16.0 * (plus_one + minus_one) - (plus_two + minus_two) - 30.0 * centre) * (1.0 / 12.0)


def library_kernel(means, rims, stress, library, slopes):
    level = pl.program_id(0)
    lane = lax.broadcasted_iota(jnp.int32, (ROWS, CY), 1)
    results = []
    for f in range(2):
        field = means[level, f]
        rim = rims[level, f]
        near = [
            turn(jnp.where(lane < 2, rim, field), -2),
            turn(jnp.where(lane < 1, rim, field), -1),
            turn(jnp.where(lane >= CY - 1, rim, field), 1),
            turn(jnp.where(lane >= CY - 2, rim, field), 2),
        ]
        slopes[f] = first_form(*near)
        bend_y = second_form(near[0], near[1], field, near[2], near[3])[4:4 + CX]

        def row(step):
            return means[level, f, pl.ds(4 + step, CX)]

        def slope_row(step):
            return slopes[f, pl.ds(4 + step, CX)]

        centre = row(0)
        along = [row(2), row(1), row(-1), row(-2)]
        grad_x = first_form(*along)
        bend_x = second_form(along[0], along[1], centre, along[2], along[3])
        cross = first_form(slope_row(2), slope_row(1), slope_row(-1), slope_row(-2))
        results.append((centre, grad_x, slope_row(0), bend_x, cross, bend_y))
    east, ux, uy, uxx, uxy, uyy = results[0]
    north, vx, vy, vxx, vxy, vyy = results[1]
    stress[0, 0] = means[level, 2, pl.ds(4, CX)] - east * east
    stress[1, 0] = means[level, 3, pl.ds(4, CX)] - east * north
    stress[2, 0] = means[level, 4, pl.ds(4, CX)] - north * north
    spin = vx - uy
    features = [ux, uy, vx, vy, uxx, uxy, uyy, vxx, vxy, vyy, vxx - uxy, vxy - uyy]
    for n, feature in enumerate(features):
        library[4 * n, 0] = feature
        library[4 * n + 1, 0] = east * feature
        library[4 * n + 2, 0] = north * feature
        library[4 * n + 3, 0] = spin * feature


def outputs(means, rims):
    whole = pl.BlockSpec(memory_space=pltpu.VMEM)
    return pl.pallas_call(
        library_kernel,
        grid=(LEV,),
        out_shape=(
            jax.ShapeDtypeStruct((3, LEV, CX, CY), jnp.float32),
            jax.ShapeDtypeStruct((48, LEV, CX, CY), jnp.float32),
        ),
        in_specs=[whole, whole],
        out_specs=(
            pl.BlockSpec((3, 1, CX, CY), lambda l: (0, l, 0, 0)),
            pl.BlockSpec((48, 1, CX, CY), lambda l: (0, l, 0, 0)),
        ),
        scratch_shapes=[pltpu.VMEM((2, ROWS, CY), jnp.float32)],
        compiler_params=pltpu.CompilerParams(vmem_limit_bytes=32 * 1024 * 1024),
        name="stress_and_library",
    )(means, rims)


def per_device(east_flow, north_flow):
    means, rims = filtered(east_flow, north_flow)
    return outputs(means, rims)


def solution(mesh):
    return jax.shard_map(
        per_device,
        mesh=mesh,
        in_specs=(P(None, "gx", "gy"), P(None, "gx", "gy")),
        out_specs=(P(None, None, "gx", "gy"), P(None, None, "gx", "gy")),
        check_vma=False,
    )
```

time: 119 us -> 25.1 us (0.21)
  waiting for transfers between devices: 52.2 us -> 0 us
  Pallas kernels: 0 us -> 24.4 us
  matrix products: 21.7 us -> 0 us
  local copies, waits for them, and re-layouts: 17 us -> 0 us
  starting transfers between devices: 15.2 us -> 0 us
  other arithmetic: 10.8 us -> 0 us
    ppermute x8 -> x0, waiting for transfers between devices: 52.2 us -> none  [the longest x4 40.8 us: with_halo(): lax.ppermute(lax.slice_in_dim(block, block.shape[dim] - width, None, axis...]
    pallas_call x0 -> x2, Pallas kernels: none -> 24.4 us  [the longest x1 19.9 us: filtered(): pl.pallas_call(filter_kernel, out_shape=(jax.ShapeDtypeStruct((LEV, 5, RO...]
    dot_general x2 -> x0, matrix products: 21.7 us -> none  [the longest x1 18.2 us: smooth_rows(): jnp.einsum('cp,flpq->flcq', matrix, fields, precision=lax.Precision.HIGHEST)]
    ppermute x8 -> x0, starting transfers between devices: 15.2 us -> none  [the longest x4 8.98 us: with_halo(): lax.ppermute(lax.slice_in_dim(block, 0, width, axis=dim), axis, backward)]
    unnamed x24 -> x0, local copies, waits for them, and re-layouts: 6.23 us -> none
    slice x5 -> x0, local copies, waits for them, and re-layouts: 6.11 us -> none  [the longest x4 3.27 us: with_halo(): lax.slice_in_dim(block, block.shape[dim] - width, None, axis=dim)]
    ppermute x2 -> x0, local copies, waits for them, and re-layouts: 4.68 us -> none  [the longest x1 2.39 us: with_halo(): lax.ppermute(lax.slice_in_dim(block, block.shape[dim] - width, None, axis...]
    slice x1 -> x0, other arithmetic: 4.18 us -> none  [with_halo(): lax.slice_in_dim(block, block.shape[dim] - width, None, axis=dim)]
  transfers between devices with their start and end apart: 8 -> 0, of which waited for: 7 -> 0; matrix products, arithmetic and copies ran while one was open for 5% -> 0% of each run, Pallas kernels for 0% -> 0%
where the time goes in v1:
time: 25.1 us; the launch traced here: 25 us
  Pallas kernels  24.4 us (97%)
  between operations  0.64 us (3%)
    pallas_call x1, Pallas kernels, filtered(): pl.pallas_call(filter_kernel, out_shape=(jax.ShapeDtypeStruct((LEV, 5, RO...  19.9 us
    pallas_call x1, Pallas kernels, outputs(): pl.pallas_call(library_kernel, grid=(LEV,), out_shape=(jax.ShapeDtypeStru...  4.5 us

profile of v1, /device:TPU:1, one launch (start us, length us, event | category | flops | bytes accessed | tf_op | source)
XLA Modules:
  0.0 25.0 jit_solution(8050560470122440597)
XLA Ops:
  0.6 19.9 %filter_and_exchange.1 = (f32[8,5,40,128]{3,2,1,0:T(8,128)S(1)}, f32[8,2,40,128]{3,2,1,0:T(8,128)S(1)}) custom-call(f32[8,128,512]{2,1,0:T(8,128)} %east.1, f32[8,128,512]{2,1,0:T(8,128)} %north.1, bf16[80,256]{1,0:T(8,128)(2,1)} %constant.4.clone.rows_hbm, bf16[2,256,256]{2,1,0:T(8,128)(2,1)} %constant.5.clone.cols_hbm), custom_call_target="tpu_custom_call" | custom-call | tf_op jit(solution)/shard_map/filter_and_exchange/pallas_call | solution.py:257
  20.5 4.5 %stress_and_library.1 = (f32[3,8,32,128]{3,2,1,0:T(8,128)}, f32[48,8,32,128]{3,2,1,0:T(8,128)}) custom-call(f32[8,5,40,128]{3,2,1,0:T(8,128)S(1)} %get-tuple-element.4.means, f32[8,2,40,128]{3,2,1,0:T(8,128)S(1)} %get-tuple-element.5.rims), custom_call_target="tpu_custom_call" | custom-call | tf_op jit(solution)/shard_map/stress_and_library/pallas_call | solution.py:346

commit v2 on v1

v2 whole, which is shorter than its diff:
```python
import jax
import jax.numpy as jnp
import ml_dtypes
import numpy as np
from jax import lax
from jax.experimental import pallas as pl
from jax.experimental.pallas import tpu as pltpu
from jax.sharding import PartitionSpec as P

spread_cells = 5.5
MESH = pl.DeviceIdType.MESH

LEV, FX, FY = 8, 128, 512
CX, CY = FX // 4, FY // 4
ROWS = CX + 8
PAIR = 2
CHUNKS = LEV // PAIR
COMBOS = 5 * PAIR
TILES = 8
AHEAD = 2


def gauss_taps():
    offsets = np.arange(33, dtype=np.float32) - np.float32(16.0)
    bumps = np.exp(np.float32(-0.5) * (offsets / np.float32(spread_cells)) ** 2)
    return (bumps / np.sum(bumps)).astype(np.float32)


def two_pieces(values):
    high = values.astype(ml_dtypes.bfloat16)
    low = (values - high.astype(np.float32)).astype(ml_dtypes.bfloat16)
    return high, low


def row_factor():
    taps = gauss_taps()
    band = np.zeros((ROWS, FX), np.float32)
    for at in range(ROWS):
        for p in range(FX):
            lag = p - 4 * (at - 4) + 16
            if 0 <= lag <= 32:
                band[at, p] = taps[lag]
    high, low = two_pieces(band)
    return np.concatenate(
        [np.concatenate([high, high], axis=1), np.concatenate([low, low], axis=1)], axis=0
    )


def column_factor():
    taps = gauss_taps()
    half = FY // 2
    blocks = []
    for part in range(2):
        band = np.zeros((half, CY), np.float32)
        for c in range(-4, CY + 4):
            for p in range(half):
                lag = p + part * half - 4 * c + 16
                if 0 <= lag <= 32:
                    band[p, c % CY] = taps[lag]
        high, low = two_pieces(band)
        blocks.append(np.concatenate([high, low], axis=1))
    return np.stack(blocks, axis=0)


def split(values):
    high = values.astype(jnp.bfloat16)
    low = (values - high.astype(jnp.float32)).astype(jnp.bfloat16)
    return high, low


def turn(values, lanes):
    return pltpu.roll(values, lanes % CY, 1)


def filter_kernel(
    east, north, rows_hbm, cols_hbm, means, edges, from_y, from_c, from_x,
    fine, rows_w, cols_w, half_done, to_y, to_x,
    load_sem, send_sem, recv_sem,
):
    def load(level, which):
        source = east if which == 0 else north
        return pltpu.make_async_copy(
            source.at[level], fine.at[which, level], load_sem.at[which, level]
        )

    rows_copy = pltpu.make_async_copy(rows_hbm, rows_w, load_sem.at[0, LEV])
    cols_copy = pltpu.make_async_copy(cols_hbm, cols_w, load_sem.at[1, LEV])
    load(0, 0).start()
    load(0, 1).start()
    rows_copy.start()
    cols_copy.start()
    for level in range(1, LEV):
        load(level, 0).start()
        load(level, 1).start()

    here_x, here_y = lax.axis_index("gx"), lax.axis_index("gy")
    count_x, count_y = lax.axis_size("gx"), lax.axis_size("gy")
    up, down = lax.rem(here_x + 1, count_x), lax.rem(here_x + count_x - 1, count_x)
    right, left = lax.rem(here_y + 1, count_y), lax.rem(here_y + count_y - 1, count_y)
    neighbours = [
        (down, here_y), (up, here_y), (here_x, right), (here_x, left),
        (down, right), (up, right), (down, left), (up, left),
    ]

    barrier = pltpu.get_barrier_semaphore()
    for neighbour in neighbours:
        pl.semaphore_signal(barrier, inc=1, device_id=neighbour, device_id_type=MESH)

    def sends(k):
        pieces = [
            (to_x.at[k, 0], from_x.at[k, 0]),
            (to_x.at[k, 1], from_x.at[k, 1]),
            (to_y.at[k, 0], from_y.at[k, 0]),
            (to_y.at[k, 1], from_y.at[k, 1]),
            (to_y.at[k, 0, pl.ds(0, 8)], from_c.at[k, 0]),
            (to_y.at[k, 0, pl.ds(CX, 8)], from_c.at[k, 1]),
            (to_y.at[k, 1, pl.ds(0, 8)], from_c.at[k, 2]),
            (to_y.at[k, 1, pl.ds(CX, 8)], from_c.at[k, 3]),
        ]
        return [
            pltpu.make_async_remote_copy(
                src_ref=source, dst_ref=target,
                send_sem=send_sem.at[k, n], recv_sem=recv_sem.at[k, n],
                device_id=neighbours[n], device_id_type=MESH,
            )
            for n, (source, target) in enumerate(pieces)
        ]

    def start_sends(k):
        for copy in sends(k):
            copy.start()

    rows_copy.wait()
    cols_copy.wait()

    lane = lax.broadcasted_iota(jnp.int32, (ROWS, CY), 1)
    group = lane // 8
    spot = lane % 8
    sub = lax.broadcasted_iota(jnp.int32, (8, CY), 0)

    def chunk(k):
        for j in range(PAIR):
            level = PAIR * k + j
            load(level, 0).wait()
            load(level, 1).wait()
            for half in range(2):
                at = pl.ds(half * (FY // 2), FY // 2)
                u = fine[0, level, :, at]
                v = fine[1, level, :, at]
                for f, values in enumerate((u, v, u * u, u * v, v * v)):
                    high, low = split(values)
                    both = jnp.dot(
                        rows_w[...], jnp.concatenate([high, low], axis=0),
                        preferred_element_type=jnp.float32,
                    )
                    half_done[pl.ds((5 * j + f) * ROWS, ROWS), at] = both[:ROWS] + both[ROWS:]
        parts = []
        for part in range(2):
            high, low = split(half_done[:, part * (FY // 2):(part + 1) * (FY // 2)])
            weights = cols_w[part]
            both = jnp.dot(
                jnp.concatenate([high, low], axis=1),
                jnp.concatenate([weights, weights], axis=0),
                preferred_element_type=jnp.float32,
            )
            parts.append(both[:, :CY] + both[:, CY:])
        packed_main = jnp.zeros((ROWS, CY), jnp.float32)
        packed_edge = jnp.zeros((ROWS, CY), jnp.float32)
        for n in range(COMBOS):
            j, f = n // 5, n % 5
            first = parts[0][n * ROWS:(n + 1) * ROWS]
            second = parts[1][n * ROWS:(n + 1) * ROWS]
            main = jnp.where(lane < CY - 4, first, 0.0) + jnp.where(lane >= 4, second, 0.0)
            edge = jnp.where(lane >= CY // 2, first, second)
            means[PAIR * k + j, f] = main
            packed_edge = jnp.where(group == n, turn(edge, 8 * n + 4), packed_edge)
            if f < 2:
                packed_main = jnp.where(group == n, turn(main, 8 * n + 4), packed_main)
        edges[k] = packed_edge
        to_y[k, 0] = jnp.where(spot >= 4, packed_edge, packed_main)
        to_y[k, 1] = jnp.where(spot < 4, packed_edge, packed_main)
        for side in range(2):
            at = side * CX
            keep = (sub < 4) if side == 0 else (sub >= 4)

            def rows_of(j, f):
                return means[PAIR * k + j, f, pl.ds(at, 8)]

            for j in range(PAIR):
                to_x[k, side, 2 * j] = rows_of(j, 0)
                to_x[k, side, 2 * j + 1] = rows_of(j, 1)
                to_x[k, side, 4 + j] = jnp.where(
                    keep, rows_of(j, 2), pltpu.roll(rows_of(j, 3), 4, 0)
                )
            to_x[k, side, 6] = jnp.where(keep, rows_of(0, 4), pltpu.roll(rows_of(1, 4), 4, 0))
            to_x[k, side, 7] = packed_edge[at:at + 8]

    def chunk_only(k, carry):
        chunk(k)
        return carry

    def chunk_and_send(k, carry):
        chunk(k)
        start_sends(k)
        return carry

    lax.fori_loop(0, AHEAD, chunk_only, 0)
    pl.semaphore_wait(barrier, len(neighbours))
    for k in range(AHEAD):
        start_sends(k)
    lax.fori_loop(AHEAD, CHUNKS, chunk_and_send, 0)

    def finish(k, carry):
        for copy in sends(k):
            copy.wait()
        return carry

    lax.fori_loop(0, CHUNKS, finish, 0)


def filtered(east_flow, north_flow):
    dma = pltpu.SemaphoreType.DMA
    f32, bf16 = jnp.float32, jnp.bfloat16
    shapes = (
        (LEV, 5, ROWS, CY), (CHUNKS, ROWS, CY),
        (CHUNKS, 2, ROWS, CY), (CHUNKS, 4, 8, CY), (CHUNKS, 2, TILES, 8, CY),
    )
    return pl.pallas_call(
        filter_kernel,
        out_shape=tuple(jax.ShapeDtypeStruct(shape, f32) for shape in shapes),
        in_specs=[pl.BlockSpec(memory_space=pltpu.HBM)] * 4,
        out_specs=(pl.BlockSpec(memory_space=pltpu.VMEM),) * len(shapes),
        scratch_shapes=[
            pltpu.VMEM((2, LEV, FX, FY), f32),
            pltpu.VMEM((2 * ROWS, 2 * FX), bf16),
            pltpu.VMEM((2, FY // 2, 2 * CY), bf16),
            pltpu.VMEM((COMBOS * ROWS, FY), f32),
            pltpu.VMEM((CHUNKS, 2, ROWS, CY), f32),
            pltpu.VMEM((CHUNKS, 2, TILES, 8, CY), f32),
            dma((2, LEV + 1)),
            dma((CHUNKS, 8)),
            dma((CHUNKS, 8)),
        ],
        compiler_params=pltpu.CompilerParams(
            collective_id=0, has_side_effects=True, vmem_limit_bytes=32 * 1024 * 1024
        ),
        name="filter_and_exchange",
    )(
        *[
            pltpu.with_memory_space_constraint(array, pltpu.HBM)
            for array in (
                east_flow, north_flow, jnp.asarray(row_factor()), jnp.asarray(column_factor())
            )
        ]
    )


def first_form(plus_two, plus_one, minus_one, minus_two):
    return (8.0 * (plus_one - minus_one) - (plus_two - minus_two)) * (1.0 / 12.0)


def second_form(plus_two, plus_one, centre, minus_one, minus_two):
    return (16.0 * (plus_one + minus_one) - (plus_two + minus_two) - 30.0 * centre) * (1.0 / 12.0)


def library_kernel(
    means, edges, from_y, from_c, from_x, stress, library, full, slopes, made_s, made_l, sem
):
    lane = lax.broadcasted_iota(jnp.int32, (ROWS, CY), 1)
    near = (lane % 8) >= 4
    inside = (lane < 4) | (lane >= CY - 4)

    def stores(level):
        return (
            pltpu.make_async_copy(made_s.at[level], stress.at[:, level], sem.at[0, level]),
            pltpu.make_async_copy(made_l.at[level], library.at[:, level], sem.at[1, level]),
        )

    def ends(first, last):
        middle = jnp.zeros((CX - 8, CY), jnp.float32)
        return jnp.concatenate([first, middle, last], axis=0)

    def chunk(k, carry):
        from_left = from_y[k, 0] + ends(from_c[k, 1], from_c[k, 0])
        from_right = from_y[k, 1] + ends(from_c[k, 3], from_c[k, 2])
        own = edges[k] + ends(from_x[k, 1, 7], from_x[k, 0, 7])
        inward = jnp.where(near, from_left, from_right)
        outward = jnp.where(near, from_right, from_left) + own
        for j in range(PAIR):
            level = PAIR * k + j
            for f in range(5):
                slot = 2 * j + f if f < 2 else (4 + j if f < 4 else 6)
                first, last = from_x[k, 1, slot], from_x[k, 0, slot]
                if f == 3 or (f == 4 and j == 1):
                    first, last = pltpu.roll(first, 4, 0), pltpu.roll(last, 4, 0)
                n = 5 * j + f
                full[f] = (
                    means[level, f]
                    + jnp.where(inside, turn(inward, -8 * n - 4), 0.0)
                    + ends(first, last)
                )
            results = []
            for f in range(2):
                field = full[f]
                rim = turn(outward, -8 * (5 * j + f) - 4)
                side = [
                    turn(jnp.where(lane < 2, rim, field), -2),
                    turn(jnp.where(lane < 1, rim, field), -1),
                    turn(jnp.where(lane >= CY - 1, rim, field), 1),
                    turn(jnp.where(lane >= CY - 2, rim, field), 2),
                ]
                slopes[f] = first_form(*side)
                bend_y = second_form(side[0], side[1], field, side[2], side[3])[4:4 + CX]

                def row(step):
                    return full[f, pl.ds(4 + step, CX)]

                def slope_row(step):
                    return slopes[f, pl.ds(4 + step, CX)]

                centre = row(0)
                along = [row(2), row(1), row(-1), row(-2)]
                grad_x = first_form(*along)
                bend_x = second_form(along[0], along[1], centre, along[2], along[3])
                cross = first_form(slope_row(2), slope_row(1), slope_row(-1), slope_row(-2))
                results.append((centre, grad_x, slope_row(0), bend_x, cross, bend_y))
            east, ux, uy, uxx, uxy, uyy = results[0]
            north, vx, vy, vxx, vxy, vyy = results[1]
            made_s[level, 0] = full[2, pl.ds(4, CX)] - east * east
            made_s[level, 1] = full[3, pl.ds(4, CX)] - east * north
            made_s[level, 2] = full[4, pl.ds(4, CX)] - north * north
            spin = vx - uy
            features = [ux, uy, vx, vy, uxx, uxy, uyy, vxx, vxy, vyy, vxx - uxy, vxy - uyy]
            for n, feature in enumerate(features):
                made_l[level, 4 * n] = feature
                made_l[level, 4 * n + 1] = east * feature
                made_l[level, 4 * n + 2] = north * feature
                made_l[level, 4 * n + 3] = spin * feature
            for copy in stores(level):
                copy.start()
        return carry

    lax.fori_loop(0, CHUNKS, chunk, 0)

    def finish(level, carry):
        for copy in stores(level):
            copy.wait()
        return carry

    lax.fori_loop(0, LEV, finish, 0)


def outputs(*arrays):
    f32 = jnp.float32
    return pl.pallas_call(
        library_kernel,
        out_shape=(
            jax.ShapeDtypeStruct((3, LEV, CX, CY), f32),
            jax.ShapeDtypeStruct((48, LEV, CX, CY), f32),
        ),
        in_specs=[pl.BlockSpec(memory_space=pltpu.VMEM)] * len(arrays),
        out_specs=(pl.BlockSpec(memory_space=pltpu.HBM),) * 2,
        scratch_shapes=[
            pltpu.VMEM((5, ROWS, CY), f32),
            pltpu.VMEM((2, ROWS, CY), f32),
            pltpu.VMEM((LEV, 3, CX, CY), f32),
            pltpu.VMEM((LEV, 48, CX, CY), f32),
            pltpu.SemaphoreType.DMA((2, LEV)),
        ],
        compiler_params=pltpu.CompilerParams(vmem_limit_bytes=32 * 1024 * 1024),
        name="stress_and_library",
    )(*arrays)


def per_device(east_flow, north_flow):
    return outputs(*filtered(east_flow, north_flow))


def solution(mesh):
    return jax.shard_map(
        per_device,
        mesh=mesh,
        in_specs=(P(None, "gx", "gy"), P(None, "gx", "gy")),
        out_specs=(P(None, None, "gx", "gy"), P(None, None, "gx", "gy")),
        check_vma=False,
    )
```

time: 25.1 us -> 21.8 us (0.87)
  Pallas kernels: 24.4 us -> 21.1 us
    pallas_call x2, Pallas kernels: 24.4 us -> 21.1 us  [the longest x1 17.9 us: filtered(): pl.pallas_call(filter_kernel, out_shape=tuple((jax.ShapeDtypeStruct(shape...]
where the time goes in v2:
time: 21.8 us; the launch traced here: 21.7 us
  Pallas kernels  21.1 us (97%)
  between operations  0.64 us (3%)
    pallas_call x1, Pallas kernels, filtered(): pl.pallas_call(filter_kernel, out_shape=tuple((jax.ShapeDtypeStruct(shape...  17.9 us
    pallas_call x1, Pallas kernels, outputs(): pl.pallas_call(library_kernel, out_shape=(jax.ShapeDtypeStruct((3, LEV, C...  3.18 us

profile of v2, /device:TPU:1, one launch (start us, length us, event | category | flops | bytes accessed | tf_op | source)
XLA Modules:
  0.0 21.7 jit_solution(1896910540870552986)
XLA Ops:
  0.6 17.9 %filter_and_exchange.1 = (f32[8,5,40,128]{3,2,1,0:T(8,128)S(1)}, f32[4,40,128]{2,1,0:T(8,128)S(1)}, f32[4,2,40,128]{3,2,1,0:T(8,128)S(1)}, f32[4,4,8,128]{3,2,1,0:T(8,128)S(1)}, f32[4,2,8,8,128]{4,3,2,1,0:T(8,128)S(1)}) custom-call(f32[8,128,512]{2,1,0:T(8,128)} %east.1, f32[8,128,512]{2,1,0:T(8,128)} %north.1, bf16[80,256]{1,0:T(8,128)(2,1)} %constant.4.clone.rows_hbm, ...), custom_call_target="tpu_custom_call" | custom-call | tf_op jit(solution)/shard_map/filter_and_exchange/pallas_call | solution.py:228
  18.5 3.2 %stress_and_library.1 = (f32[3,8,32,128]{3,2,1,0:T(8,128)}, f32[48,8,32,128]{3,2,1,0:T(8,128)}) custom-call(f32[8,5,40,128]{3,2,1,0:T(8,128)S(1)} %get-tuple-element.7.means, f32[4,40,128]{2,1,0:T(8,128)S(1)} %get-tuple-element.8.edges, f32[4,2,40,128]{3,2,1,0:T(8,128)S(1)} %get-tuple-element.9.from_y, f32[4,4,8,128]{3,2,1,0:T(8,128)S(1)} %get-tuple-element.10.from_c, ...), custom_call_target="tpu_custom_call" | custom-call | tf_op jit(solution)/shard_map/stress_and_library/pallas_call | solution.py:355

commit v3 on v2

--- a/solution.py
+++ b/solution.py
@@ -17,7 +17,8 @@
 CHUNKS = LEV // PAIR
 COMBOS = 5 * PAIR
 TILES = 8
-AHEAD = 2
+AHEAD = 0
+EARLY_Z = 2
 
 
 def gauss_taps():
@@ -48,17 +49,18 @@
 
 def column_factor():
     taps = gauss_taps()
-    half = FY // 2
+    edge, half = FY // 4, FY // 2
     blocks = []
-    for part in range(2):
-        band = np.zeros((half, CY), np.float32)
+    for start, count in ((0, edge), (FY - edge, edge), (edge, half)):
+        band = np.zeros((count, CY), np.float32)
         for c in range(-4, CY + 4):
-            for p in range(half):
-                lag = p + part * half - 4 * c + 16
+            for p in range(count):
+                lag = p + start - 4 * c + 16
                 if 0 <= lag <= 32:
                     band[p, c % CY] = taps[lag]
         high, low = two_pieces(band)
-        blocks.append(np.concatenate([high, low], axis=1))
+        both = np.concatenate([high, low], axis=1)
+        blocks.append(both if count == half else np.concatenate([both, both], axis=0))
     return np.stack(blocks, axis=0)
 
 
@@ -74,61 +76,86 @@
 
 def filter_kernel(
     east, north, rows_hbm, cols_hbm, means, edges, from_y, from_c, from_x,
-    fine, rows_w, cols_w, half_done, to_y, to_x,
-    load_sem, send_sem, recv_sem,
+    sides, middle, rows_w, cols_w, half_done, to_y, to_x,
+    load_sem, weight_sem, y_send, y_recv, x_send, x_recv,
 ):
-    def load(level, which):
-        source = east if which == 0 else north
-        return pltpu.make_async_copy(
-            source.at[level], fine.at[which, level], load_sem.at[which, level]
-        )
-
-    rows_copy = pltpu.make_async_copy(rows_hbm, rows_w, load_sem.at[0, LEV])
-    cols_copy = pltpu.make_async_copy(cols_hbm, cols_w, load_sem.at[1, LEV])
-    load(0, 0).start()
-    load(0, 1).start()
-    rows_copy.start()
-    cols_copy.start()
-    for level in range(1, LEV):
-        load(level, 0).start()
-        load(level, 1).start()
-
     here_x, here_y = lax.axis_index("gx"), lax.axis_index("gy")
     count_x, count_y = lax.axis_size("gx"), lax.axis_size("gy")
     up, down = lax.rem(here_x + 1, count_x), lax.rem(here_x + count_x - 1, count_x)
     right, left = lax.rem(here_y + 1, count_y), lax.rem(here_y + count_y - 1, count_y)
-    neighbours = [
-        (down, here_y), (up, here_y), (here_x, right), (here_x, left),
-        (down, right), (up, right), (down, left), (up, left),
-    ]
+    corners = [(down, right), (up, right), (down, left), (up, left)]
+    along_y = [(here_x, right), (here_x, left)]
+    along_x = [(down, here_y), (up, here_y)]
+    neighbours = corners + along_y + along_x
 
     barrier = pltpu.get_barrier_semaphore()
     for neighbour in neighbours:
         pl.semaphore_signal(barrier, inc=1, device_id=neighbour, device_id_type=MESH)
 
-    def sends(k):
+    quarter = FY // 4
+
+    def load(k, which, piece):
+        source = (east if which == 0 else north).at[pl.ds(PAIR * k, PAIR)]
+        levels = pl.ds(PAIR * k, PAIR)
+        if piece == 0:
+            source = source.at[:, :, pl.ds(0, quarter)]
+            target = sides.at[which, levels, :, pl.ds(0, quarter)]
+        elif piece == 1:
+            source = source.at[:, :, pl.ds(3 * quarter, quarter)]
+            target = sides.at[which, levels, :, pl.ds(quarter, quarter)]
+        else:
+            source = source.at[:, :, pl.ds(quarter, 2 * quarter)]
+            target = middle.at[which, levels]
+        return pltpu.make_async_copy(source, target, load_sem.at[k, which, piece])
+
+    def start_loads(k, pieces):
+        for which in range(2):
+            for piece in pieces:
+                load(k, which, piece).start()
+
+    def wait_loads(k, pieces):
+        for which in range(2):
+            for piece in pieces:
+                load(k, which, piece).wait()
+
+    rows_copy = pltpu.make_async_copy(rows_hbm, rows_w, weight_sem.at[0])
+    cols_copy = pltpu.make_async_copy(cols_hbm, cols_w, weight_sem.at[1])
+    start_loads(0, (0, 1))
+    rows_copy.start()
+    cols_copy.start()
+    for k in range(1, CHUNKS):
+        start_loads(k, (0, 1))
+    for k in range(CHUNKS):
+        start_loads(k, (2,))
+
+    def remote(source, target, send, recv, device):
+        return pltpu.make_async_remote_copy(
+            src_ref=source, dst_ref=target, send_sem=send, recv_sem=recv,
+            device_id=device, device_id_type=MESH,
+        )
+
+    def sends_y():
+        last = ROWS // 8 - 1
         pieces = [
-            (to_x.at[k, 0], from_x.at[k, 0]),
-            (to_x.at[k, 1], from_x.at[k, 1]),
-            (to_y.at[k, 0], from_y.at[k, 0]),
-            (to_y.at[k, 1], from_y.at[k, 1]),
-            (to_y.at[k, 0, pl.ds(0, 8)], from_c.at[k, 0]),
-            (to_y.at[k, 0, pl.ds(CX, 8)], from_c.at[k, 1]),
-            (to_y.at[k, 1, pl.ds(0, 8)], from_c.at[k, 2]),
-            (to_y.at[k, 1, pl.ds(CX, 8)], from_c.at[k, 3]),
+            (to_y.at[0, 0], from_c.at[0]),
+            (to_y.at[0, last], from_c.at[1]),
+            (to_y.at[1, 0], from_c.at[2]),
+            (to_y.at[1, last], from_c.at[3]),
+            (to_y.at[0], from_y.at[0]),
+            (to_y.at[1], from_y.at[1]),
         ]
         return [
-            pltpu.make_async_remote_copy(
-                src_ref=source, dst_ref=target,
-                send_sem=send_sem.at[k, n], recv_sem=recv_sem.at[k, n],
-                device_id=neighbours[n], device_id_type=MESH,
-            )
+            remote(source, target, y_send.at[n], y_recv.at[n], neighbours[n])
             for n, (source, target) in enumerate(pieces)
         ]
 
-    def start_sends(k):
-        for copy in sends(k):
-            copy.start()
+    def sends_x(k):
+        return [
+            remote(
+                to_x.at[k, n], from_x.at[k, n], x_send.at[k, n], x_recv.at[k, n], along_x[n]
+            )
+            for n in range(2)
+        ]
 
     rows_copy.wait()
     cols_copy.wait()
@@ -138,38 +165,37 @@
     spot = lane % 8
     sub = lax.broadcasted_iota(jnp.int32, (8, CY), 0)
 
-    def chunk(k):
+    def rows_first(k, fine):
         for j in range(PAIR):
             level = PAIR * k + j
-            load(level, 0).wait()
-            load(level, 1).wait()
-            for half in range(2):
-                at = pl.ds(half * (FY // 2), FY // 2)
-                u = fine[0, level, :, at]
-                v = fine[1, level, :, at]
-                for f, values in enumerate((u, v, u * u, u * v, v * v)):
-                    high, low = split(values)
-                    both = jnp.dot(
-                        rows_w[...], jnp.concatenate([high, low], axis=0),
-                        preferred_element_type=jnp.float32,
-                    )
-                    half_done[pl.ds((5 * j + f) * ROWS, ROWS), at] = both[:ROWS] + both[ROWS:]
-        parts = []
-        for part in range(2):
-            high, low = split(half_done[:, part * (FY // 2):(part + 1) * (FY // 2)])
-            weights = cols_w[part]
-            both = jnp.dot(
-                jnp.concatenate([high, low], axis=1),
-                jnp.concatenate([weights, weights], axis=0),
-                preferred_element_type=jnp.float32,
-            )
-            parts.append(both[:, :CY] + both[:, CY:])
+            u = fine[0, level]
+            v = fine[1, level]
+            for f, values in enumerate((u, v, u * u, u * v, v * v)):
+                high, low = split(values)
+                both = jnp.dot(
+                    rows_w[...], jnp.concatenate([high, low], axis=0),
+                    preferred_element_type=jnp.float32,
+                )
+                half_done[pl.ds((5 * j + f) * ROWS, ROWS), :] = both[:ROWS] + both[ROWS:]
+
+    def columns(values, weights):
+        high, low = split(values)
+        both = jnp.dot(
+            jnp.concatenate([high, low], axis=1), weights, preferred_element_type=jnp.float32
+        )
+        return both[:, :CY] + both[:, CY:]
+
+    def side_chunk(k, carry):
+        wait_loads(k, (0, 1))
+        rows_first(k, sides)
+        from_low = columns(half_done[:, :quarter], cols_w[0])
+        from_high = columns(half_done[:, quarter:], cols_w[1])
         packed_main = jnp.zeros((ROWS, CY), jnp.float32)
         packed_edge = jnp.zeros((ROWS, CY), jnp.float32)
         for n in range(COMBOS):
             j, f = n // 5, n % 5
-            first = parts[0][n * ROWS:(n + 1) * ROWS]
-            second = parts[1][n * ROWS:(n + 1) * ROWS]
+            first = from_low[n * ROWS:(n + 1) * ROWS]
+            second = from_high[n * ROWS:(n + 1) * ROWS]
             main = jnp.where(lane < CY - 4, first, 0.0) + jnp.where(lane >= 4, second, 0.0)
             edge = jnp.where(lane >= CY // 2, first, second)
             means[PAIR * k + j, f] = main
@@ -177,8 +203,19 @@
             if f < 2:
                 packed_main = jnp.where(group == n, turn(main, 8 * n + 4), packed_main)
         edges[k] = packed_edge
-        to_y[k, 0] = jnp.where(spot >= 4, packed_edge, packed_main)
-        to_y[k, 1] = jnp.where(spot < 4, packed_edge, packed_main)
+        at = pl.ds(8 * k, 8)
+        tiled = (ROWS // 8, 8, CY)
+        to_y[0, :, at] = jnp.where(spot >= 4, packed_edge, packed_main).reshape(tiled)
+        to_y[1, :, at] = jnp.where(spot < 4, packed_edge, packed_main).reshape(tiled)
+        return carry
+
+    def middle_chunk(k):
+        wait_loads(k, (2,))
+        rows_first(k, middle)
+        inner = columns(half_done[...], jnp.concatenate([cols_w[2], cols_w[2]], axis=0))
+        for n in range(COMBOS):
+            j, f = n // 5, n % 5
+            means[PAIR * k + j, f] += inner[n * ROWS:(n + 1) * ROWS]
         for side in range(2):
             at = side * CX
             keep = (sub < 4) if side == 0 else (sub >= 4)
@@ -193,37 +230,46 @@
                     keep, rows_of(j, 2), pltpu.roll(rows_of(j, 3), 4, 0)
                 )
             to_x[k, side, 6] = jnp.where(keep, rows_of(0, 4), pltpu.roll(rows_of(1, 4), 4, 0))
-            to_x[k, side, 7] = packed_edge[at:at + 8]
-
-    def chunk_only(k, carry):
-        chunk(k)
-        return carry
-
-    def chunk_and_send(k, carry):
-        chunk(k)
-        start_sends(k)
-        return carry
-
-    lax.fori_loop(0, AHEAD, chunk_only, 0)
+            to_x[k, side, 7] = edges[k, pl.ds(at, 8)]
+
+    def middle_only(k, carry):
+        middle_chunk(k)
+        return carry
+
+    def middle_and_send(k, carry):
+        middle_chunk(k)
+        for copy in sends_x(k):
+            copy.start()
+        return carry
+
+    def send_only(k, carry):
+        for copy in sends_x(k):
+            copy.start()
+        return carry
+
+    ahead = jnp.where(lax.rem(here_y, 8) < EARLY_Z, CHUNKS, AHEAD)
+    lax.fori_loop(0, CHUNKS, side_chunk, 0)
+    lax.fori_loop(0, ahead, middle_only, 0)
     pl.semaphore_wait(barrier, len(neighbours))
-    for k in range(AHEAD):
-        start_sends(k)
-    lax.fori_loop(AHEAD, CHUNKS, chunk_and_send, 0)
-
-    def finish(k, carry):
-        for copy in sends(k):
+    for copy in sends_y():
+        copy.start()
+    lax.fori_loop(0, ahead, send_only, 0)
+    lax.fori_loop(ahead, CHUNKS, middle_and_send, 0)
+
+    for k in range(CHUNKS):
+        for copy in sends_x(k):
             copy.wait()
-        return carry
-
-    lax.fori_loop(0, CHUNKS, finish, 0)
+    for copy in sends_y():
+        copy.wait()
 
 
 def filtered(east_flow, north_flow):
     dma = pltpu.SemaphoreType.DMA
     f32, bf16 = jnp.float32, jnp.bfloat16
+    tiles = ROWS // 8
     shapes = (
         (LEV, 5, ROWS, CY), (CHUNKS, ROWS, CY),
-        (CHUNKS, 2, ROWS, CY), (CHUNKS, 4, 8, CY), (CHUNKS, 2, TILES, 8, CY),
+        (2, tiles, CHUNKS * 8, CY), (4, CHUNKS * 8, CY), (CHUNKS, 2, TILES, 8, CY),
     )
     return pl.pallas_call(
         filter_kernel,
@@ -231,15 +277,19 @@
         in_specs=[pl.BlockSpec(memory_space=pltpu.HBM)] * 4,
         out_specs=(pl.BlockSpec(memory_space=pltpu.VMEM),) * len(shapes),
         scratch_shapes=[
-            pltpu.VMEM((2, LEV, FX, FY), f32),
+            pltpu.VMEM((2, LEV, FX, FY // 2), f32),
+            pltpu.VMEM((2, LEV, FX, FY // 2), f32),
             pltpu.VMEM((2 * ROWS, 2 * FX), bf16),
-            pltpu.VMEM((2, FY // 2, 2 * CY), bf16),
-            pltpu.VMEM((COMBOS * ROWS, FY), f32),
-            pltpu.VMEM((CHUNKS, 2, ROWS, CY), f32),
+            pltpu.VMEM((3, FY // 2, 2 * CY), bf16),
+            pltpu.VMEM((COMBOS * ROWS, FY // 2), f32),
+            pltpu.VMEM((2, tiles, CHUNKS * 8, CY), f32),
             pltpu.VMEM((CHUNKS, 2, TILES, 8, CY), f32),
-            dma((2, LEV + 1)),
-            dma((CHUNKS, 8)),
-            dma((CHUNKS, 8)),
+            dma((CHUNKS, 2, 3)),
+            dma((2,)),
+            dma((6,)),
+            dma((6,)),
+            dma((CHUNKS, 2)),
+            dma((CHUNKS, 2)),
         ],
         compiler_params=pltpu.CompilerParams(
             collective_id=0, has_side_effects=True, vmem_limit_bytes=32 * 1024 * 1024
@@ -281,8 +331,9 @@
         return jnp.concatenate([first, middle, last], axis=0)
 
     def chunk(k, carry):
-        from_left = from_y[k, 0] + ends(from_c[k, 1], from_c[k, 0])
-        from_right = from_y[k, 1] + ends(from_c[k, 3], from_c[k, 2])
+        at = pl.ds(8 * k, 8)
+        from_left = from_y[0, :, at].reshape(ROWS, CY) + ends(from_c[1, at], from_c[0, at])
+        from_right = from_y[1, :, at].reshape(ROWS, CY) + ends(from_c[3, at], from_c[2, at])
         own = edges[k] + ends(from_x[k, 1, 7], from_x[k, 0, 7])
         inward = jnp.where(near, from_left, from_right)
         outward = jnp.where(near, from_right, from_left) + own

time: 21.8 us -> 20.4 us (0.936)
  Pallas kernels: 21.1 us -> 19.7 us
    pallas_call x1, Pallas kernels: 17.9 us -> 16.5 us  [filtered(): pl.pallas_call(filter_kernel, out_shape=tuple((jax.ShapeDtypeStruct(shape...]
where the time goes in v3:
time: 20.4 us; the launch traced here: 20.3 us
  Pallas kernels  19.7 us (97%)
  between operations  0.64 us (3%)
    pallas_call x1, Pallas kernels, filtered(): pl.pallas_call(filter_kernel, out_shape=tuple((jax.ShapeDtypeStruct(shape...  16.5 us
    pallas_call x1, Pallas kernels, outputs(): pl.pallas_call(library_kernel, out_shape=(jax.ShapeDtypeStruct((3, LEV, C...  3.18 us

profile of v3, /device:TPU:1, one launch (start us, length us, event | category | flops | bytes accessed | tf_op | source)
XLA Modules:
  0.0 20.3 jit_solution(12749579425055850492)
XLA Ops:
  0.6 16.5 %filter_and_exchange.1 = (f32[8,5,40,128]{3,2,1,0:T(8,128)S(1)}, f32[4,40,128]{2,1,0:T(8,128)S(1)}, f32[2,5,32,128]{3,2,1,0:T(8,128)S(1)}, f32[4,32,128]{2,1,0:T(8,128)S(1)}, f32[4,2,8,8,128]{4,3,2,1,0:T(8,128)S(1)}) custom-call(f32[8,128,512]{2,1,0:T(8,128)} %east.1, f32[8,128,512]{2,1,0:T(8,128)} %north.1, bf16[80,256]{1,0:T(8,128)(2,1)} %constant.4.clone.rows_hbm, ...), custom_call_target="tpu_custom_call" | custom-call | tf_op jit(solution)/shard_map/filter_and_exchange/pallas_call | solution.py:274
  17.1 3.2 %stress_and_library.1 = (f32[3,8,32,128]{3,2,1,0:T(8,128)}, f32[48,8,32,128]{3,2,1,0:T(8,128)}) custom-call(f32[8,5,40,128]{3,2,1,0:T(8,128)S(1)} %get-tuple-element.7.means, f32[4,40,128]{2,1,0:T(8,128)S(1)} %get-tuple-element.8.edges, f32[2,5,32,128]{3,2,1,0:T(8,128)S(1)} %get-tuple-element.9.from_y, f32[4,32,128]{2,1,0:T(8,128)S(1)} %get-tuple-element.10.from_c, ...), custom_call_target="tpu_custom_call" | custom-call | tf_op jit(solution)/shard_map/stress_and_library/pallas_call | solution.py:406

commit v4 on v3

--- a/solution.py
+++ b/solution.py
@@ -16,9 +16,12 @@
 PAIR = 2
 CHUNKS = LEV // PAIR
 COMBOS = 5 * PAIR
-TILES = 8
-AHEAD = 0
-EARLY_Z = 2
+TILES = 6
+AHEAD = 1
+
+
+def slot_of(j, f):
+    return 2 * j + f if f < 2 else 4 + 3 * j + f - 2
 
 
 def gauss_taps():
@@ -75,23 +78,10 @@
 
 
 def filter_kernel(
-    east, north, rows_hbm, cols_hbm, means, edges, from_y, from_c, from_x,
-    sides, middle, rows_w, cols_w, half_done, to_y, to_x,
+    east, north, rows_hbm, cols_hbm, means, edges, from_y, from_c, from_x, from_e,
+    sides, middle, rows_w, cols_w, half_done, to_y, to_x, to_e,
     load_sem, weight_sem, y_send, y_recv, x_send, x_recv,
 ):
-    here_x, here_y = lax.axis_index("gx"), lax.axis_index("gy")
-    count_x, count_y = lax.axis_size("gx"), lax.axis_size("gy")
-    up, down = lax.rem(here_x + 1, count_x), lax.rem(here_x + count_x - 1, count_x)
-    right, left = lax.rem(here_y + 1, count_y), lax.rem(here_y + count_y - 1, count_y)
-    corners = [(down, right), (up, right), (down, left), (up, left)]
-    along_y = [(here_x, right), (here_x, left)]
-    along_x = [(down, here_y), (up, here_y)]
-    neighbours = corners + along_y + along_x
-
-    barrier = pltpu.get_barrier_semaphore()
-    for neighbour in neighbours:
-        pl.semaphore_signal(barrier, inc=1, device_id=neighbour, device_id_type=MESH)
-
     quarter = FY // 4
 
     def load(k, which, piece):
@@ -123,6 +113,21 @@
     start_loads(0, (0, 1))
     rows_copy.start()
     cols_copy.start()
+    here_x, here_y = lax.axis_index("gx"), lax.axis_index("gy")
+    count_x, count_y = lax.axis_size("gx"), lax.axis_size("gy")
+    up = jnp.where(here_x == count_x - 1, 0, here_x + 1)
+    down = jnp.where(here_x == 0, count_x - 1, here_x - 1)
+    right = jnp.where(here_y == count_y - 1, 0, here_y + 1)
+    left = jnp.where(here_y == 0, count_y - 1, here_y - 1)
+    corners = [(down, right), (up, right), (down, left), (up, left)]
+    along_y = [(here_x, right), (here_x, left)]
+    along_x = [(down, here_y), (up, here_y)]
+    neighbours = corners + along_y + along_x
+
+    barrier = pltpu.get_barrier_semaphore()
+    for neighbour in neighbours:
+        pl.semaphore_signal(barrier, inc=1, device_id=neighbour, device_id_type=MESH)
+
     for k in range(1, CHUNKS):
         start_loads(k, (0, 1))
     for k in range(CHUNKS):
@@ -143,6 +148,8 @@
             (to_y.at[1, last], from_c.at[3]),
             (to_y.at[0], from_y.at[0]),
             (to_y.at[1], from_y.at[1]),
+            (to_e.at[0], from_e.at[0]),
+            (to_e.at[1], from_e.at[1]),
         ]
         return [
             remote(source, target, y_send.at[n], y_recv.at[n], neighbours[n])
@@ -192,10 +199,11 @@
         from_high = columns(half_done[:, quarter:], cols_w[1])
         packed_main = jnp.zeros((ROWS, CY), jnp.float32)
         packed_edge = jnp.zeros((ROWS, CY), jnp.float32)
-        for n in range(COMBOS):
-            j, f = n // 5, n % 5
-            first = from_low[n * ROWS:(n + 1) * ROWS]
-            second = from_high[n * ROWS:(n + 1) * ROWS]
+        for at in range(COMBOS):
+            j, f = at // 5, at % 5
+            n = slot_of(j, f)
+            first = from_low[at * ROWS:(at + 1) * ROWS]
+            second = from_high[at * ROWS:(at + 1) * ROWS]
             main = jnp.where(lane < CY - 4, first, 0.0) + jnp.where(lane >= 4, second, 0.0)
             edge = jnp.where(lane >= CY // 2, first, second)
             means[PAIR * k + j, f] = main
@@ -205,6 +213,10 @@
         edges[k] = packed_edge
         at = pl.ds(8 * k, 8)
         tiled = (ROWS // 8, 8, CY)
+        quarter_lanes = lax.broadcasted_iota(jnp.int32, (8, CY), 1) // 32
+        for side in range(2):
+            turned = pltpu.roll(packed_edge[side * CX:side * CX + 8], 32 * k, 1)
+            to_e[side] = jnp.where(quarter_lanes == k, turned, to_e[side])
         to_y[0, :, at] = jnp.where(spot >= 4, packed_edge, packed_main).reshape(tiled)
         to_y[1, :, at] = jnp.where(spot < 4, packed_edge, packed_main).reshape(tiled)
         return carry
@@ -223,14 +235,17 @@
             def rows_of(j, f):
                 return means[PAIR * k + j, f, pl.ds(at, 8)]
 
+            last = rows_of(1, 1)
+            for at_slot, (j, f) in enumerate(((0, 0), (0, 1), (1, 0))):
+                spare = pltpu.roll(last, 6 - 2 * at_slot, 0)
+                to_x[k, side, at_slot] = jnp.where(
+                    (sub < 6) if side == 0 else (sub >= 2), rows_of(j, f), spare
+                )
             for j in range(PAIR):
-                to_x[k, side, 2 * j] = rows_of(j, 0)
-                to_x[k, side, 2 * j + 1] = rows_of(j, 1)
-                to_x[k, side, 4 + j] = jnp.where(
+                to_x[k, side, 3 + j] = jnp.where(
                     keep, rows_of(j, 2), pltpu.roll(rows_of(j, 3), 4, 0)
                 )
-            to_x[k, side, 6] = jnp.where(keep, rows_of(0, 4), pltpu.roll(rows_of(1, 4), 4, 0))
-            to_x[k, side, 7] = edges[k, pl.ds(at, 8)]
+            to_x[k, side, 5] = jnp.where(keep, rows_of(0, 4), pltpu.roll(rows_of(1, 4), 4, 0))
 
     def middle_only(k, carry):
         middle_chunk(k)
@@ -247,7 +262,8 @@
             copy.start()
         return carry
 
-    ahead = jnp.where(lax.rem(here_y, 8) < EARLY_Z, CHUNKS, AHEAD)
+    ahead = AHEAD
+    to_e[...] = jnp.zeros_like(to_e)
     lax.fori_loop(0, CHUNKS, side_chunk, 0)
     lax.fori_loop(0, ahead, middle_only, 0)
     pl.semaphore_wait(barrier, len(neighbours))
@@ -270,6 +286,7 @@
     shapes = (
         (LEV, 5, ROWS, CY), (CHUNKS, ROWS, CY),
         (2, tiles, CHUNKS * 8, CY), (4, CHUNKS * 8, CY), (CHUNKS, 2, TILES, 8, CY),
+        (2, 8, CY),
     )
     return pl.pallas_call(
         filter_kernel,
@@ -284,10 +301,11 @@
             pltpu.VMEM((COMBOS * ROWS, FY // 2), f32),
             pltpu.VMEM((2, tiles, CHUNKS * 8, CY), f32),
             pltpu.VMEM((CHUNKS, 2, TILES, 8, CY), f32),
+            pltpu.VMEM((2, 8, CY), f32),
             dma((CHUNKS, 2, 3)),
             dma((2,)),
-            dma((6,)),
-            dma((6,)),
+            dma((8,)),
+            dma((8,)),
             dma((CHUNKS, 2)),
             dma((CHUNKS, 2)),
         ],
@@ -314,10 +332,11 @@
 
 
 def library_kernel(
-    means, edges, from_y, from_c, from_x, stress, library, full, slopes, made_s, made_l, sem
+    means, edges, from_y, from_c, from_x, from_e, stress, library, full, slopes, made_s, made_l, sem
 ):
     lane = lax.broadcasted_iota(jnp.int32, (ROWS, CY), 1)
     near = (lane % 8) >= 4
+    sub = lax.broadcasted_iota(jnp.int32, (8, CY), 0)
     inside = (lane < 4) | (lane >= CY - 4)
 
     def stores(level):
@@ -334,17 +353,32 @@
         at = pl.ds(8 * k, 8)
         from_left = from_y[0, :, at].reshape(ROWS, CY) + ends(from_c[1, at], from_c[0, at])
         from_right = from_y[1, :, at].reshape(ROWS, CY) + ends(from_c[3, at], from_c[2, at])
-        own = edges[k] + ends(from_x[k, 1, 7], from_x[k, 0, 7])
+        back = lax.rem(CY - 32 * k, CY)
+        own = edges[k] + ends(pltpu.roll(from_e[1], back, 1), pltpu.roll(from_e[0], back, 1))
         inward = jnp.where(near, from_left, from_right)
         outward = jnp.where(near, from_right, from_left) + own
         for j in range(PAIR):
             level = PAIR * k + j
             for f in range(5):
-                slot = 2 * j + f if f < 2 else (4 + j if f < 4 else 6)
-                first, last = from_x[k, 1, slot], from_x[k, 0, slot]
-                if f == 3 or (f == 4 and j == 1):
-                    first, last = pltpu.roll(first, 4, 0), pltpu.roll(last, 4, 0)
-                n = 5 * j + f
+                if f < 2 and (j, f) != (1, 1):
+                    first, last = from_x[k, 1, 2 * j + f], from_x[k, 0, 2 * j + f]
+                elif f < 2:
+                    first, last = [
+                        jnp.where(
+                            sub < low, pltpu.roll(from_x[k, side, 0], 2, 0),
+                            jnp.where(
+                                sub < low + 2, pltpu.roll(from_x[k, side, 1], 4, 0),
+                                pltpu.roll(from_x[k, side, 2], 6, 0),
+                            ),
+                        )
+                        for side, low in ((1, 4), (0, 2))
+                    ]
+                else:
+                    slot = 3 + j if f < 4 else 5
+                    first, last = from_x[k, 1, slot], from_x[k, 0, slot]
+                    if f == 3 or (f == 4 and j == 1):
+                        first, last = pltpu.roll(first, 4, 0), pltpu.roll(last, 4, 0)
+                n = slot_of(j, f)
                 full[f] = (
                     means[level, f]
                     + jnp.where(inside, turn(inward, -8 * n - 4), 0.0)
@@ -353,7 +387,7 @@
             results = []
             for f in range(2):
                 field = full[f]
-                rim = turn(outward, -8 * (5 * j + f) - 4)
+                rim = turn(outward, -8 * slot_of(j, f) - 4)
                 side = [
                     turn(jnp.where(lane < 2, rim, field), -2),
                     turn(jnp.where(lane < 1, rim, field), -1),

time: 20.4 us -> 20.2 us (level)
    pallas_call x1, Pallas kernels: 16.5 us -> 16.2 us  [filtered(): pl.pallas_call(filter_kernel, out_shape=tuple((jax.ShapeDtypeStruct(shape...]
where the time goes in v4:
time: 20.2 us; the launch traced here: 20.1 us
  Pallas kernels  19.5 us (97%)
  between operations  0.64 us (3%)
    pallas_call x1, Pallas kernels, filtered(): pl.pallas_call(filter_kernel, out_shape=tuple((jax.ShapeDtypeStruct(shape...  16.2 us
    pallas_call x1, Pallas kernels, outputs(): pl.pallas_call(library_kernel, out_shape=(jax.ShapeDtypeStruct((3, LEV, C...  3.24 us

profile of v4, /device:TPU:1, one launch (start us, length us, event | category | flops | bytes accessed | tf_op | source)
XLA Modules:
  0.0 20.1 jit_solution(15318009776385243469)
XLA Ops:
  0.6 16.2 %filter_and_exchange.1 = (f32[8,5,40,128]{3,2,1,0:T(8,128)S(1)}, f32[4,40,128]{2,1,0:T(8,128)S(1)}, f32[2,5,32,128]{3,2,1,0:T(8,128)S(1)}, f32[4,32,128]{2,1,0:T...) custom-call(f32[8,128,512]{2,1,0:T(8,128)} %east.1, f32[8,128,512]{2,1,0:T(8,128)} %north.1, ...), custom_call_target="tpu_custom_call" | custom-call | tf_op jit(solution)/shard_map/filter_and_exchange/pallas_call | solution.py:291
  16.9 3.2 %stress_and_library.1 = (f32[3,8,32,128]{3,2,1,0:T(8,128)}, f32[48,8,32,128]{3,2,1,0:T(8,128)}) custom-call(f32[8,5,40,128]{3,2,1,0:T(8,128)S(1)} %get-tuple-element.8.means, f32[4,40,128]{2,1,0:T(8,128)S(1)} %get-tuple-element.9.edges, f32[2,5,32,128]{3,2,1,0:T(8,128)S(1)} %get-tuple-element.10.from_y, f32[4,32,128]{2,1,0:T(8,128)S(1)} %get-tuple-element.11.from_c, ...), custom_call_target="tpu_custom_call" | custom-call | tf_op jit(solution)/shard_map/stress_and_library/pallas_call | solution.py:440

commit v5 on v4

--- a/solution.py
+++ b/solution.py
@@ -267,9 +267,12 @@
     lax.fori_loop(0, CHUNKS, side_chunk, 0)
     lax.fori_loop(0, ahead, middle_only, 0)
     pl.semaphore_wait(barrier, len(neighbours))
-    for copy in sends_y():
+    copies = sends_y()
+    for copy in copies[:4]:
         copy.start()
     lax.fori_loop(0, ahead, send_only, 0)
+    for copy in copies[4:]:
+        copy.start()
     lax.fori_loop(ahead, CHUNKS, middle_and_send, 0)
 
     for k in range(CHUNKS):

time: 20.2 us -> 20.2 us (level)
  no operation moved by 1% of the time
where the time goes in v5:
time: 20.2 us; the launch traced here: 20.1 us
  Pallas kernels  19.5 us (97%)
  between operations  0.64 us (3%)
    pallas_call x1, Pallas kernels, filtered(): pl.pallas_call(filter_kernel, out_shape=tuple((jax.ShapeDtypeStruct(shape...  16.2 us
    pallas_call x1, Pallas kernels, outputs(): pl.pallas_call(library_kernel, out_shape=(jax.ShapeDtypeStruct((3, LEV, C...  3.24 us

profile of v5, /device:TPU:1, one launch (start us, length us, event | category | flops | bytes accessed | tf_op | source)
XLA Modules:
  0.0 20.1 jit_solution(17585730747309670918)
XLA Ops:
  0.6 16.2 %filter_and_exchange.1 = (f32[8,5,40,128]{3,2,1,0:T(8,128)S(1)}, f32[4,40,128]{2,1,0:T(8,128)S(1)}, f32[2,5,32,128]{3,2,1,0:T(8,128)S(1)}, f32[4,32,128]{2,1,0:T...) custom-call(f32[8,128,512]{2,1,0:T(8,128)} %east.1, f32[8,128,512]{2,1,0:T(8,128)} %north.1, ...), custom_call_target="tpu_custom_call" | custom-call | tf_op jit(solution)/shard_map/filter_and_exchange/pallas_call | solution.py:294
  16.9 3.2 %stress_and_library.1 = (f32[3,8,32,128]{3,2,1,0:T(8,128)}, f32[48,8,32,128]{3,2,1,0:T(8,128)}) custom-call(f32[8,5,40,128]{3,2,1,0:T(8,128)S(1)} %get-tuple-element.8.means, f32[4,40,128]{2,1,0:T(8,128)S(1)} %get-tuple-element.9.edges, f32[2,5,32,128]{3,2,1,0:T(8,128)S(1)} %get-tuple-element.10.from_y, f32[4,32,128]{2,1,0:T(8,128)S(1)} %get-tuple-element.11.from_c, ...), custom_call_target="tpu_custom_call" | custom-call | tf_op jit(solution)/shard_map/stress_and_library/pallas_call | solution.py:443
